TPU v7x, 32 devices: a whole 2x2x4 slice. The times are simulated.
32 devices in a mesh: wide: 8 (over z, x), narrow: 4 (over y, core).
Axes of the slice: x: 2, y: 2, z: 4, core: 2. Of those that a mesh axis runs over, the one named last changes fastest.
Arguments:
- tokens: bfloat16 [32, 512, 768], P(('wide', 'narrow')), may hold values from -6 to 6
- query_weight: bfloat16 [768, 768], P('wide'), may hold values from -0.0546875 to 0.0546875
- key_weight: bfloat16 [768, 768], P('wide'), may hold values from -0.21875 to 0.21875
- value_weight: bfloat16 [768, 768], P('wide'), may hold values from -0.21875 to 0.21875
- output_weight: bfloat16 [768, 768], P('wide'), may hold values from -1.25 to 1.25
- expand_weight: bfloat16 [768, 3072], P('wide'), may hold values from -0.21875 to 0.21875
- contract_weight: bfloat16 [3072, 768], P('wide'), may hold values from -0.109375 to 0.109375
- attention_gain: float32 [768], replicated, may hold values from 0.5 to 1.5
- feedforward_gain: float32 [768], replicated, may hold values from 0.5 to 1.5
- bias_table: float32 [32, 12], replicated, may hold values from -4 to 4
- query_length: int32 [32], P(('wide', 'narrow')), may hold values from 4 to 64, as said below
- passage_length: int32 [32], P(('wide', 'narrow')), may hold values from 252 to 508, as said below
- pair_order: int32 [32], replicated, may hold values from 0 to 31, as said below
- regrouped_grad: bfloat16 [32, 512, 768], P('narrow', 'wide'), may hold values from -6 to 6
Outputs:
- regrouped: bfloat16 [32, 512, 768], P('narrow', 'wide')
- tokens_grad: float32 [32, 512, 768], P(('wide', 'narrow'))
- query_weight_grad: float32 [768, 768], P('wide')
- key_weight_grad: float32 [768, 768], P('wide')
- value_weight_grad: float32 [768, 768], P('wide')
- output_weight_grad: float32 [768, 768], P('wide')
- expand_weight_grad: float32 [768, 3072], P('wide')
- contract_weight_grad: float32 [3072, 768], P('wide')
- attention_gain_grad: float32 [768], replicated
- feedforward_gain_grad: float32 [768], replicated
- bias_table_grad: float32 [32, 12], replicated
Inputs may be any that keep to these rules, and one draw needn't show every extreme that they name: query_length + passage_length lies between half of 512 and 512; in every draw some pair has exactly 512 and some pair exactly half of 512. `passage_length`: see query_length. `pair_order`: a permutation of the 32 pairs; the pair at place k has an index r with (r) % 4 equal to k // 8.
All inputs are finite; a program needn't handle non-finite values.
Results may differ from a plain program's by a relative error of at most 0.015.
Values may be sent and summed in bfloat16 or wider, within the bound.
No kernel may reach another device: no remote copies, remote signals or barrier semaphores. Data moves between devices by JAX's collectives and lax.ppermute only.
A program may use at most 192 MiB of HBM per device.

v0:
```python
import jax
import jax.numpy as jnp
import numpy as np
from jax import lax
from jax.sharding import PartitionSpec as P

MAX_DIST = 128


epsilon = 1e-06
negative = -1000000000.0


def bucket_index(offset_values, bucket_total, max_reach):
    exact_part = bucket_total // 4
    bounds_table = np.ceil(
        exact_part * (max_reach / exact_part) ** (np.arange(1, exact_part) / exact_part) - 1e-06
    ).astype(np.int32)
    distance = jnp.abs(offset_values)
    passed = jnp.zeros_like(distance)
    for limit_value in bounds_table:
        passed = passed + (distance >= int(limit_value)).astype(jnp.int32)
    coarse = jnp.where(distance < exact_part, distance, exact_part + passed)
    return coarse + (offset_values > 0).astype(jnp.int32) * (bucket_total // 2)


def rms_norm(values, gain_values):
    return (
        values
        * lax.rsqrt(jnp.mean(values * values, axis=-1, keepdims=True) + epsilon)
        * gain_values
    )


def toeplitz_rows(table_line, length):
    padded = jnp.concatenate([table_line, jnp.zeros((1,), table_line.dtype)])
    tiled = jnp.tile(padded, length + 1)
    window = lax.slice_in_dim(tiled, length - 1, length - 1 + length * (2 * length - 1))
    return window.reshape(length, 2 * length - 1)[:, :length]


def diagonal_sums(matrix):
    length = matrix.shape[0]
    flipped = matrix[::-1]
    padded = jnp.concatenate([flipped, jnp.zeros_like(flipped)], axis=1)
    flat = padded.reshape(-1)[: length * (2 * length - 1)]
    return jnp.sum(flat.reshape(length, 2 * length - 1), axis=0)


def transposed_product(left, right):
    return lax.dot_general(
        left, right, (((0,), (0,)), ((), ())), preferred_element_type=jnp.float32
    )


def right_product(left, right):
    return lax.dot_general(
        left, right, (((1,), (1,)), ((), ())), preferred_element_type=jnp.float32
    )


def on_device(
    tokens,
    query_weight,
    key_weight,
    value_weight,
    output_weight,
    expand_weight,
    contract_weight,
    attention_gain,
    feedforward_gain,
    bias_table,
    query_length,
    passage_length,
    pair_order,
    regrouped_grad,
):
    row_count, length, width = tokens.shape
    head_count = bias_table.shape[1]
    head_size = width // head_count
    bucket_count = bias_table.shape[0]
    token_count = row_count * length
    full_query, full_key, full_value, full_output, full_expand, full_contract = (
        lax.all_gather(query_weight, "wide", axis=0, tiled=True),
        lax.all_gather(key_weight, "wide", axis=0, tiled=True),
        lax.all_gather(value_weight, "wide", axis=0, tiled=True),
        lax.all_gather(output_weight, "wide", axis=0, tiled=True),
        lax.all_gather(expand_weight, "wide", axis=0, tiled=True),
        lax.all_gather(contract_weight, "wide", axis=0, tiled=True),
    )
    pair_total = query_length + passage_length
    positions = jnp.arange(length, dtype=jnp.int32)
    key_fill = jnp.where(positions[None, :] < pair_total[:, None], 0.0, negative).astype(
        jnp.float32
    )
    offsets = jnp.arange(2 * length - 1, dtype=jnp.int32) - (length - 1)
    bucket_ids = bucket_index(offsets, bucket_count, MAX_DIST)
    one_hot = (bucket_ids[:, None] == jnp.arange(bucket_count, dtype=jnp.int32)[None, :]).astype(
        jnp.float32
    )
    bias_lines = jnp.dot(one_hot, bias_table, precision=lax.Precision.HIGHEST).T

    def split_heads(matrix):
        return matrix.reshape(row_count, length, head_count, head_size).transpose(2, 0, 1, 3)

    def join_heads(stacked):
        return stacked.transpose(1, 2, 0, 3).reshape(token_count, width)

    def head_scores(query_head, key_head, bias_line):
        bias_square = toeplitz_rows(bias_line, length)
        raw_scores = jnp.einsum(
            "rqd,rkd->rqk", query_head, key_head, preferred_element_type=jnp.float32
        )
        return raw_scores + bias_square[None] + key_fill[:, None, :]

    def head_forward(head_items):
        query_head, key_head, value_head, bias_line = head_items
        scores = head_scores(query_head, key_head, bias_line)
        peak = jnp.max(scores, axis=-1, keepdims=True)
        weights_exp = jnp.exp(scores - peak)
        total = jnp.sum(weights_exp, axis=-1, keepdims=True)
        probs_low = (weights_exp / total).astype(jnp.bfloat16)
        head_mixed = jnp.einsum(
            "rqk,rkd->rqd", probs_low, value_head, preferred_element_type=jnp.float32
        )
        return (head_mixed, peak[..., 0] + jnp.log(total[..., 0]))

    def head_backward(head_items):
        query_head, key_head, value_head, grad_head, logsum_head, bias_line = head_items
        scores = head_scores(query_head, key_head, bias_line)
        probs = jnp.exp(scores - logsum_head[..., None])
        probs_low = probs.astype(jnp.bfloat16)
        grad_value_head = jnp.einsum(
            "rqk,rqd->rkd", probs_low, grad_head, preferred_element_type=jnp.float32
        )
        grad_probs = jnp.einsum(
            "rqd,rkd->rqk", grad_head, value_head, preferred_element_type=jnp.float32
        )
        grad_scores = probs * (grad_probs - jnp.sum(probs * grad_probs, axis=-1, keepdims=True))
        scores_low = grad_scores.astype(jnp.bfloat16)
        grad_query_head = jnp.einsum(
            "rqk,rkd->rqd", scores_low, key_head, preferred_element_type=jnp.float32
        )
        grad_key_head = jnp.einsum(
            "rqk,rqd->rkd", scores_low, query_head, preferred_element_type=jnp.float32
        )
        bias_line_grad = diagonal_sums(jnp.sum(scores_low.astype(jnp.float32), axis=0))
        return (
            grad_query_head.astype(jnp.bfloat16),
            grad_key_head.astype(jnp.bfloat16),
            grad_value_head.astype(jnp.bfloat16),
            bias_line_grad,
        )

    inputs = tokens.astype(jnp.float32).reshape(token_count, width)
    normed_one, norm_pull_one = jax.vjp(rms_norm, inputs, attention_gain)
    attention_input = normed_one.astype(jnp.bfloat16)
    queries = jnp.dot(attention_input, full_query, preferred_element_type=jnp.float32).astype(
        jnp.bfloat16
    )
    key_vectors = jnp.dot(attention_input, full_key, preferred_element_type=jnp.float32).astype(
        jnp.bfloat16
    )
    value_vectors = jnp.dot(attention_input, full_value, preferred_element_type=jnp.float32).astype(
        jnp.bfloat16
    )
    query_heads = split_heads(queries)
    key_heads = split_heads(key_vectors)
    value_heads = split_heads(value_vectors)
    head_mixed, head_logsum = lax.map(
        head_forward, (query_heads, key_heads, value_heads, bias_lines)
    )
    mixed = join_heads(head_mixed).astype(jnp.bfloat16)
    residual = inputs + jnp.dot(mixed, full_output, preferred_element_type=jnp.float32)
    normed_two, norm_pull_two = jax.vjp(rms_norm, residual, feedforward_gain)
    expand_input = normed_two.astype(jnp.bfloat16)
    pre_activation = jnp.dot(expand_input, full_expand, preferred_element_type=jnp.float32)
    activated, gelu_pull = jax.vjp(jax.nn.gelu, pre_activation)
    hidden = activated.astype(jnp.bfloat16)
    block_output = (
        residual + jnp.dot(hidden, full_contract, preferred_element_type=jnp.float32)
    ).astype(jnp.bfloat16)
    received = lax.all_to_all(
        block_output.reshape(row_count, length, width),
        "wide",
        split_axis=1,
        concat_axis=0,
        tiled=True,
    )
    narrow_index = lax.axis_index("narrow")
    narrow_count = lax.axis_size("narrow")
    group_rows = received.shape[0]
    chosen = lax.dynamic_slice_in_dim(pair_order, narrow_index * group_rows, group_rows)
    local_rows = chosen // (row_count * narrow_count) * row_count + chosen % row_count
    regrouped = jnp.take(received, local_rows, axis=0)
    arranged = jnp.zeros_like(regrouped_grad).at[local_rows].set(regrouped_grad)
    grad_block = lax.all_to_all(arranged, "wide", split_axis=0, concat_axis=1, tiled=True).reshape(
        token_count, width
    )
    contract_grad = transposed_product(hidden, grad_block)
    grad_hidden = right_product(grad_block, full_contract)
    grad_pre = gelu_pull(grad_hidden)[0].astype(jnp.bfloat16)
    expand_grad = transposed_product(expand_input, grad_pre)
    grad_expand_input = right_product(grad_pre, full_expand)
    grad_residual_part, feedforward_gain_grad = norm_pull_two(grad_expand_input)
    grad_residual = grad_block.astype(jnp.float32) + grad_residual_part
    grad_mixed_in = grad_residual.astype(jnp.bfloat16)
    output_grad = transposed_product(mixed, grad_mixed_in)
    grad_mixed = right_product(grad_mixed_in, full_output).astype(jnp.bfloat16)
    grad_query_heads, grad_key_heads, grad_value_heads, bias_line_grads = lax.map(
        head_backward,
        (query_heads, key_heads, value_heads, split_heads(grad_mixed), head_logsum, bias_lines),
    )
    grad_queries = join_heads(grad_query_heads)
    grad_keys = join_heads(grad_key_heads)
    grad_values = join_heads(grad_value_heads)
    query_grad = transposed_product(attention_input, grad_queries)
    key_grad = transposed_product(attention_input, grad_keys)
    value_grad = transposed_product(attention_input, grad_values)
    grad_attention_input = (
        right_product(grad_queries, full_query)
        + right_product(grad_keys, full_key)
        + right_product(grad_values, full_value)
    )
    grad_tokens_part, attention_gain_grad = norm_pull_one(grad_attention_input)
    tokens_grad = (grad_residual + grad_tokens_part).reshape(row_count, length, width)
    table_grad = jnp.dot(one_hot.T, bias_line_grads.T, precision=lax.Precision.HIGHEST)
    summed_query, summed_key, summed_value, summed_output, summed_expand, summed_contract = (
        lax.psum_scatter(query_grad, "wide", scatter_dimension=0, tiled=True),
        lax.psum_scatter(key_grad, "wide", scatter_dimension=0, tiled=True),
        lax.psum_scatter(value_grad, "wide", scatter_dimension=0, tiled=True),
        lax.psum_scatter(output_grad, "wide", scatter_dimension=0, tiled=True),
        lax.psum_scatter(expand_grad, "wide", scatter_dimension=0, tiled=True),
        lax.psum_scatter(contract_grad, "wide", scatter_dimension=0, tiled=True),
    )
    final_query, final_key, final_value, final_output, final_expand, final_contract = (
        lax.psum(summed_query.astype(jnp.bfloat16), "narrow").astype(jnp.float32),
        lax.psum(summed_key.astype(jnp.bfloat16), "narrow").astype(jnp.float32),
        lax.psum(summed_value.astype(jnp.bfloat16), "narrow").astype(jnp.float32),
        lax.psum(summed_output.astype(jnp.bfloat16), "narrow").astype(jnp.float32),
        lax.psum(summed_expand.astype(jnp.bfloat16), "narrow").astype(jnp.float32),
        lax.psum(summed_contract.astype(jnp.bfloat16), "narrow").astype(jnp.float32),
    )
    final_attention_gain, final_feedforward_gain, final_table = lax.psum(
        (attention_gain_grad, feedforward_gain_grad, table_grad), ("wide", "narrow")
    )
    return (
        regrouped,
        tokens_grad,
        final_query,
        final_key,
        final_value,
        final_output,
        final_expand,
        final_contract,
        final_attention_gain,
        final_feedforward_gain,
        final_table,
    )


def solution(mesh):
    in_specs = (
        P(("wide", "narrow"), None, None),
        P("wide", None),
        P("wide", None),
        P("wide", None),
        P("wide", None),
        P("wide", None),
        P("wide", None),
        P(),
        P(),
        P(),
        P(("wide", "narrow")),
        P(("wide", "narrow")),
        P(),
        P("narrow", "wide", None),
    )
    out_specs = (
        P("narrow", "wide", None),
        P(("wide", "narrow"), None, None),
        P("wide", None),
        P("wide", None),
        P("wide", None),
        P("wide", None),
        P("wide", None),
        P("wide", None),
        P(),
        P(),
        P(),
    )
    return jax.shard_map(
        on_device, mesh=mesh, in_specs=in_specs, out_specs=out_specs, check_vma=False
    )
```

profile of v0, /device:TPU:0, one launch (start us, length us, event | category | flops | bytes accessed | tf_op | source)
XLA Modules:
  0.0 1345.9 jit_solution(14554969979054969926)
XLA Ops:
  15.5 7.4 all-to-all-start.1
  25.6 32.7 %all-gather.7.cloned.1.call-done = bf16[768,768]{1,0:T(8,128)(2,1)} async-done(((bf16[96,768]{1,0:T(8,128)(2,1)}), bf16[768,768]{1,0:T(8,128)(2,1)}) %all-gather.7.cloned.1.call-update) | async-done | bytes 1179664 | tf_op jit(solution)/shard_map/all_gather | solution.py:84
  62.6 38.0 %all-gather.9.cloned.1.call-done = bf16[768,768]{1,0:T(8,128)(2,1)} async-done(((bf16[96,768]{1,0:T(8,128)(2,1)}), bf16[768,768]{1,0:T(8,128)(2,1)}) %all-gather.9.cloned.1.call-update) | async-done | bytes 1179664 | tf_op jit(solution)/shard_map/all_gather | solution.py:85
  104.6 38.0 %all-gather.11.cloned.1.call-done = bf16[768,768]{1,0:T(8,128)(2,1)} async-done(((bf16[96,768]{1,0:T(8,128)(2,1)}), bf16[768,768]{1,0:T(8,128)(2,1)}) %all-gather.11.cloned.1.call-update) | async-done | bytes 1179664 | tf_op jit(solution)/shard_map/all_gather | solution.py:86
  146.6 144.1 %while.30 = (s32[]{:T(128)}, bf16[12,1,512,64]{2,3,1,0:T(8,128)(2,1)}, f32[12,1,512]{2,1,0:T(1,128)S(1)}, bf16[12,1,512,64]{3,2,1,0:T(8,128)(2,1)}, bf16[12,1,51...) while((s32[]{:T(128)}, ...), condition=%wide.region_4.5_spmd.clone, body=%wide.region_1.4_spmd.clone.sunk | while | flops 69207552 | bytes 24692872 | solution.py:170
  150.8 2.8 reshape.375
  162.8 2.8 reshape.375
  174.7 2.8 reshape.375
  186.7 2.8 reshape.375
  198.7 2.8 reshape.375
  210.7 2.8 reshape.375
  223.1 2.8 reshape.375
  235.0 2.8 reshape.375
  247.0 2.8 reshape.375
  259.0 2.8 reshape.375
  271.0 2.8 reshape.375
  283.0 2.8 reshape.375
  293.2 8.4 fusion.103
  301.6 43.8 %all-gather.15.cloned.1.call-done = bf16[768,3072]{1,0:T(8,128)(2,1)} async-done(((bf16[96,3072]{1,0:T(8,128)(2,1)}), bf16[768,3072]{1,0:T(8,128)(2,1)}) %all-gather.15.cloned.1.call-update) | async-done | bytes 4718608 | tf_op jit(solution)/shard_map/all_gather | solution.py:88
  345.4 12.9 fusion.53
  358.4 2.8 multiply_reduce_fusion.1
  366.1 285.0 %while.31 = (s32[]{:T(128)}, bf16[12,1,512,64]{2,3,1,0:T(8,128)(2,1)}, bf16[12,1,512,64]{2,3,1,0:T(8,128)(2,1)}, bf16[12,1,512,64]{2,3,1,0:T(8,128)(2,1)}, f32[1...) while((s32[]{:T(128)}, ...), condition=%wide.region_11.12_spmd.clone, body=%wide.region_8.11_spmd.clone.sunk | while | flops 170754048 | bytes 47170740 | solution.py:210
  386.6 3.0 reshape.377
  410.3 3.0 reshape.377
  434.1 3.0 reshape.377
  457.8 3.0 reshape.377
  481.6 3.0 reshape.377
  505.3 3.0 reshape.377
  529.1 3.0 reshape.377
  552.9 3.0 reshape.377
  576.6 3.0 reshape.377
  600.4 3.0 reshape.377
  624.1 3.0 reshape.377
  647.9 3.0 reshape.377
  651.1 3.7 fusion.96
  665.9 8.8 fusion.90
  675.0 9.9 fusion.101
  685.5 8.4 fusion.70
  696.8 6.6 reduce.6
  704.5 3.6 all-to-all-start
  714.5 20.2 %reduce-scatter.7.cloned.1.call-done = f32[96,768]{1,0:T(8,128)} async-done(((f32[768,768]{1,0:T(8,128)}), f32[96,768]{1,0:T(8,128)}) %reduce-scatter.7.cloned.1.call-update) | async-done | bytes 294928 | tf_op jit(solution)/shard_map/reduce_scatter | solution.py:229
  736.3 68.7 %reduce-scatter.9.cloned.1.call-done = f32[96,768]{1,0:T(8,128)} async-done(((f32[768,768]{1,0:T(8,128)}), f32[96,768]{1,0:T(8,128)}) %reduce-scatter.9.cloned.1.call-update) | async-done | bytes 294928 | tf_op jit(solution)/shard_map/reduce_scatter | solution.py:230
  806.7 69.9 %reduce-scatter.11.cloned.1.call-done = f32[96,768]{1,0:T(8,128)} async-done(((f32[768,768]{1,0:T(8,128)}), f32[96,768]{1,0:T(8,128)}) %reduce-scatter.11.cloned.1.call-update) | async-done | bytes 294928 | tf_op jit(solution)/shard_map/reduce_scatter | solution.py:231
  878.3 69.7 %reduce-scatter.13.cloned.1.call-done = f32[96,768]{1,0:T(8,128)} async-done(((f32[768,768]{1,0:T(8,128)}), f32[96,768]{1,0:T(8,128)}) %reduce-scatter.13.cloned.1.call-update) | async-done | bytes 294928 | tf_op jit(solution)/shard_map/reduce_scatter | solution.py:232
  949.6 164.3 %reduce-scatter.15.cloned.1.call-done = f32[96,3072]{1,0:T(8,128)} async-done(((f32[768,3072]{1,0:T(8,128)}), f32[96,3072]{1,0:T(8,128)}) %reduce-scatter.15.cloned.1.call-update) | async-done | bytes 1179664 | tf_op jit(solution)/shard_map/reduce_scatter | solution.py:233
  1116.1 163.7 %reduce-scatter.17.cloned.1.call-done = f32[384,768]{1,0:T(8,128)} async-done(((f32[3072,768]{1,0:T(8,128)}), f32[384,768]{1,0:T(8,128)}) %reduce-scatter.17.cloned.1.call-update) | async-done | bytes 1179664 | tf_op jit(solution)/shard_map/reduce_scatter | solution.py:234
  1282.4 40.2 %all-reduce.1 = (f32[768]{0:T(1024)}, f32[768]{0:T(1024)}, f32[32,12]{0,1:T(8,128)}) all-reduce(f32[768]{0:T(1024)S(1)} %get-tuple-element.253, f32[768]{0:T(1024)S(1)} %get-tuple-element.251, f32[32,12]{0,1:T(8,128)S(1)} %fusion.72), channel_id=1, replica_groups=mesh['wide'=8,'narrow'=4] {'wide','narrow'}, use_global_device_ids=true, to_apply=%region_26.27 | all-reduce | flops 1920 | bytes 15360 | tf_op jit(solution)/shard_map/psum | solution.py:244
  1322.6 3.0 fusion.69
  (589 shorter events, 434.2 us)
Async XLA Ops:
  7.2 18.0 %copy-start = (f32[32,12]{0,1:T(8,128)S(1)}, f32[32,12]{0,1:T(8,128)}, u32[]{:S(2)}) copy-start(f32[32,12]{0,1:T(8,128)} %param.27) | copy-start | bytes 4612
  7.2 5.6 copy-start.11
  7.2 51.2 %all-gather.7.cloned.1.call-start = ((), (), s32[]{:S(2)}) async-start(), calls=%async_computation.8 | async-start | bytes 1327104 | tf_op jit(solution)/shard_map/all_gather | solution.py:84
  7.9 92.6 %all-gather.9.cloned.1.call-start = ((), (), s32[]{:S(2)}) async-start(), calls=%async_computation.9 | async-start | bytes 1327104 | tf_op jit(solution)/shard_map/all_gather | solution.py:85
  8.7 133.9 %all-gather.11.cloned.1.call-start = ((), (), s32[]{:S(2)}) async-start(), calls=%async_computation.10 | async-start | bytes 1327104 | tf_op jit(solution)/shard_map/all_gather | solution.py:86
  9.4 281.3 %all-gather.13.cloned.1.call-start = ((), (), s32[]{:S(2)}) async-start(), calls=%async_computation.11 | async-start | bytes 1327104 | tf_op jit(solution)/shard_map/all_gather | solution.py:87
  10.0 283.2 %all-gather.17.cloned.1.call-start = ((), (), s32[]{:S(2)}) async-start(), calls=%async_computation.13 | async-start | bytes 5308416 | tf_op jit(solution)/shard_map/all_gather | solution.py:89
  11.9 3.6 copy-start.21
  15.5 8.1 copy-start.2
  15.5 42.9 %copy-start.18 = (f32[768]{0:T(1024)S(1)}, f32[768]{0:T(1024)}, u32[]{:S(2)}) copy-start(f32[768]{0:T(1024)} %param.25) | copy-start | bytes 9220
  15.5 277.7 %all-to-all-start.1 = ((bf16[8,64,768]{2,1,0:T(8,128)(2,1)}), bf16[8,64,768]{2,1,0:T(8,128)(2,1)}, u32[]{:S(2)}, u32[]{:S(2)}) async-start(bf16[8,64,768]{2,1,0:T(8,128)(2,1)} %scatter_fusion), calls=%async_computation.1 | async-start | bytes 1572864 | tf_op jit(solution)/shard_map/all_to_all | solution.py:197
  22.9 322.5 %all-gather.15.cloned.1.call-start = ((), (), s32[]{:S(2)}) async-start(), calls=%async_computation.12 | async-start | bytes 5308416 | tf_op jit(solution)/shard_map/all_gather | solution.py:88
  23.5 711.2 %reduce-scatter.7.cloned.1.call-start = ((), (), s32[]{:S(2)}) async-start(), calls=%async_computation.14 | async-start | bytes 2654208 | tf_op jit(solution)/shard_map/reduce_scatter | solution.py:229
  23.5 37.0 %copy-start.23 = (s32[1023]{0:T(1024)}, s32[1023]{0:T(1024)S(1)}, u32[]{:S(2)}) copy-start(s32[1023]{0:T(1024)S(1)} %fusion.78) | copy-start | bytes 12280
  23.8 36.7 %copy-start.19 = (f32[512]{0:T(512)}, f32[512]{0:T(512)S(1)}, u32[]{:S(2)}) copy-start(f32[512]{0:T(512)S(1)} %fusion.63) | copy-start | bytes 6148
  153.6 1.2 slice-start
  165.6 1.2 slice-start
  177.6 1.2 slice-start
  189.5 1.2 slice-start
  201.5 1.2 slice-start
  213.5 1.2 slice-start
  225.9 1.2 slice-start
  249.8 1.3 slice-start
  261.8 1.2 slice-start
  273.8 1.3 slice-start
  293.2 68.1 %copy-start.6 = (f32[512,768]{1,0:T(8,128)}, f32[512,768]{1,0:T(8,128)S(1)}, u32[]{:S(2)}) copy-start(f32[512,768]{1,0:T(8,128)S(1)} %get-tuple-element.311) | copy-start | bytes 4718596
  293.2 52.2 %copy-start.17 = (f32[768]{0:T(1024)S(1)}, f32[768]{0:T(1024)}, u32[]{:S(2)}) copy-start(f32[768]{0:T(1024)} %param.26) | copy-start | bytes 9220
  345.4 12.9 copy-start.26
  358.4 2.9 copy-start.7
  361.2 2.9 copy-start.28
  654.9 1.4 copy-start.13
  654.9 150.2 %reduce-scatter.9.cloned.1.call-start = ((), (), s32[]{:S(2)}) async-start(), calls=%async_computation.15 | async-start | bytes 2654208 | tf_op jit(solution)/shard_map/reduce_scatter | solution.py:230
  658.6 218.0 %reduce-scatter.11.cloned.1.call-start = ((), (), s32[]{:S(2)}) async-start(), calls=%async_computation.16 | async-start | bytes 2654208 | tf_op jit(solution)/shard_map/reduce_scatter | solution.py:231
  662.1 1.4 copy-start.5
  662.1 1.6 copy-start.12
  662.1 285.8 %reduce-scatter.13.cloned.1.call-start = ((), (), s32[]{:S(2)}) async-start(), calls=%async_computation.17 | async-start | bytes 2654208 | tf_op jit(solution)/shard_map/reduce_scatter | solution.py:232
  665.9 448.0 %reduce-scatter.15.cloned.1.call-start = ((), (), s32[]{:S(2)}) async-start(), calls=%async_computation.18 | async-start | bytes 10616832 | tf_op jit(solution)/shard_map/reduce_scatter | solution.py:233
  674.8 605.0 %reduce-scatter.17.cloned.1.call-start = ((), (), s32[]{:S(2)}) async-start(), calls=%async_computation.19 | async-start | bytes 10616832 | tf_op jit(solution)/shard_map/reduce_scatter | solution.py:234
  704.5 621.0 %all-to-all-start = ((bf16[8,2,24576]{2,1,0:T(2,128)(2,1)}), bf16[8,2,24576]{2,1,0:T(2,128)(2,1)S(1)}, u32[]{:S(2)}, u32[]{:S(2)}) async-start(bf16[8,2,24576]{2,1,0:T(2,128)(2,1)} %reshape.370), calls=%async_computation | async-start | bytes 1572864 | tf_op jit(solution)/shard_map/all_to_all | solution.py:183
  708.1 622.1 %all-reduce.5.cloned.1.call-start = ((), (), s32[]{:S(2)}) async-start(), calls=%async_computation.20 | async-start | bytes 3538944 | tf_op jit(solution)/shard_map/psum | solution.py:237
  708.1 2.5 copy-start.14
  708.2 2.5 copy-start.27
  710.7 1.5 copy-start.10
  1116.1 165.9 %copy-start.24 = (s32[1023]{0:T(1024)S(1)}, s32[1023]{0:T(1024)}, u32[]{:S(2)}) copy-start(s32[1023]{0:T(1024)} %copy-done.23) | copy-start | bytes 12280
  1116.1 206.5 %copy-start.20 = (f32[512]{0:T(512)S(1)}, f32[512]{0:T(512)}, u32[]{:S(2)}) copy-start(f32[512]{0:T(512)} %copy-done.19) | copy-start | bytes 6148
  1330.2 6.7 copy-start.16
  1332.0 6.1 copy-start.15
  1336.9 2.2 copy-start.1
  (20 other events, 23.1 us)
Sparse Core Ops, SparseCore 0:
  10.2 48.0 all-gather.6
  60.5 39.9 all-gather.8
  102.8 39.8 all-gather.10
  144.6 39.8 all-gather.12
  186.6 78.7 all-gather.16
  267.3 78.0 all-gather.14
  655.0 79.6 reduce-scatter.6
  738.2 66.8 reduce-scatter.8
  808.6 68.0 reduce-scatter.10
  880.0 67.9 reduce-scatter.12
  951.6 162.3 reduce-scatter.14
  1117.4 162.3 reduce-scatter.16
  1283.2 47.0 all-reduce.4
where the time goes:
time: 1350 us
  waiting for transfers between devices  715 us (53%)
  local copies, waits for them, and re-layouts  307 us (23%)
  matrix products  211 us (16%)
  other arithmetic  43.1 us (3%)
  blocking collectives  40.2 us (3%)
  between operations  15.9 us (1%)
    reduce_scatter x1, waiting for transfers between devices, on_device(): lax.psum_scatter(expand_grad, 'wide', scatter_dimension=0, tiled=True)  164 us
    reduce_scatter x1, waiting for transfers between devices, on_device(): lax.psum_scatter(contract_grad, 'wide', scatter_dimension=0, tiled=True)  164 us
    reduce_scatter x1, waiting for transfers between devices, on_device(): lax.psum_scatter(value_grad, 'wide', scatter_dimension=0, tiled=True)  69.9 us
    reduce_scatter x1, waiting for transfers between devices, on_device(): lax.psum_scatter(output_grad, 'wide', scatter_dimension=0, tiled=True)  69.7 us
    reduce_scatter x1, waiting for transfers between devices, on_device(): lax.psum_scatter(key_grad, 'wide', scatter_dimension=0, tiled=True)  68.7 us
    reshape x24, local copies, waits for them, and re-layouts, toeplitz_rows(): return window.reshape(length, 2 * length - 1)[:, :length]  66.5 us
    slice x24, local copies, waits for them, and re-layouts, toeplitz_rows(): lax.slice_in_dim(tiled, length - 1, length - 1 + length * (2 * length - 1))  53.2 us
    another operation x48, local copies, waits for them, and re-layouts, toeplitz_rows(): tiled = jnp.tile(padded, length + 1)  45.5 us
  transfers between devices with their start and end apart: 15, of which 11 were waited for; matrix products, arithmetic and copies ran while one was open for 17% of the time, Pallas kernels for 0%

commit v1 on v0

v1 whole, which is shorter than its diff:
```python
import functools

import jax
import jax.numpy as jnp
import numpy as np
from jax import lax
from jax.experimental import pallas as pl
from jax.experimental.pallas import tpu as pltpu
from jax.sharding import PartitionSpec as P

MAX_DIST = 128
epsilon = 1e-06
negative = -1000000000.0
F32 = jnp.float32
BF16 = jnp.bfloat16
MIB = 1024 * 1024


def bucket_index(offset_values, bucket_total, max_reach):
    exact_part = bucket_total // 4
    bounds_table = np.ceil(
        exact_part * (max_reach / exact_part) ** (np.arange(1, exact_part) / exact_part) - 1e-06
    ).astype(np.int32)
    distance = np.abs(offset_values)
    passed = np.zeros_like(distance)
    for limit_value in bounds_table:
        passed = passed + (distance >= int(limit_value)).astype(np.int32)
    coarse = np.where(distance < exact_part, distance, exact_part + passed)
    return coarse + (offset_values > 0).astype(np.int32) * (bucket_total // 2)


def one_hot_rows(offset_values, bucket_total):
    ids = bucket_index(np.asarray(offset_values, np.int32), bucket_total, MAX_DIST)
    return (ids[:, None] == np.arange(bucket_total)[None, :]).astype(np.float32)


def nn(left, right):
    return lax.dot_general(left, right, (((1,), (0,)), ((), ())), preferred_element_type=F32)


def nt(left, right):
    return lax.dot_general(left, right, (((1,), (1,)), ((), ())), preferred_element_type=F32)


def tn(left, right):
    return lax.dot_general(left, right, (((0,), (0,)), ((), ())), preferred_element_type=F32)


def norm_scale(values):
    return lax.rsqrt(jnp.mean(values * values, axis=-1, keepdims=True) + epsilon)


def norm_backward(values, gain, grad):
    scale = norm_scale(values)
    scaled = grad * gain
    dots = jnp.mean(scaled * values, axis=-1, keepdims=True)
    grad_values = scale * scaled - values * (scale * scale * scale * dots)
    grad_gain = jnp.sum(grad * (values * scale), axis=0, keepdims=True)
    return grad_values, grad_gain


def whole(shape):
    return pl.BlockSpec(shape, lambda *_: (0,) * len(shape))


def call(kernel, grid, in_specs, out_specs, out_shape, scratch=(), flops=0, vmem=56):
    return pl.pallas_call(
        kernel,
        grid=grid,
        in_specs=in_specs,
        out_specs=out_specs,
        out_shape=out_shape,
        scratch_shapes=list(scratch),
        compiler_params=pltpu.CompilerParams(vmem_limit_bytes=vmem * MIB),
        cost_estimate=pl.CostEstimate(flops=flops, bytes_accessed=8 * MIB, transcendentals=0),
    )


def shaped(shape, kind):
    return jax.ShapeDtypeStruct(shape, kind)


def project_kernel(tokens_ref, gain_ref, weight_ref, normed_ref, qkv_ref):
    @pl.when(pl.program_id(0) == 0)
    def _():
        values = tokens_ref[...].astype(F32)
        normed_ref[...] = (values * norm_scale(values) * gain_ref[...]).astype(BF16)

    qkv_ref[...] = nn(normed_ref[...], weight_ref[...]).astype(BF16)


def project(tokens, gain, weight):
    length, width = tokens.shape
    total = weight.shape[1]
    block = width
    return call(
        project_kernel,
        (total // block,),
        [whole((length, width)), whole((1, width)), pl.BlockSpec((width, block), lambda j: (0, j))],
        [whole((length, width)), pl.BlockSpec((length, block), lambda j: (0, j))],
        [shaped((length, width), BF16), shaped((length, total), BF16)],
        flops=2 * length * width * total,
    )(tokens, gain, weight)


QB = 256
KB = 128


def head_lanes(shape, which, size):
    lanes = lax.broadcasted_iota(jnp.int32, shape, 1)
    return (lanes < size) == (which == 0)


def attend_kernel(q_ref, k_ref, v_ref, line_ref, fill_ref, mixed_ref, probs_ref):
    length, pair = q_ref.shape
    size = pair // 2
    queries = q_ref[...]
    keys = k_ref[...]
    values_t = v_ref[...].T
    fill = fill_ref[...]
    heads = []
    for a in range(2):
        own = jnp.where(head_lanes(queries.shape, a, size), queries, jnp.zeros_like(queries))
        line = jnp.broadcast_to(line_ref[0, a : a + 1, :], (KB, 2 * length))
        band = pltpu.roll(line, 0, 1, stride=1, stride_axis=0)
        parts = []
        for qb in range(0, length, QB):
            raw = nt(keys, own[qb : qb + QB])
            rows = []
            for kb in range(0, length, KB):
                start = length - KB - kb + qb
                rows.append(
                    raw[kb : kb + KB] + (band[:, start : start + QB] + fill[kb : kb + KB])
                )
            scores = jnp.concatenate(rows, axis=0)
            peak = jnp.max(scores, axis=0, keepdims=True)
            weights = jnp.exp(scores - peak)
            total = jnp.sum(weights, axis=0, keepdims=True)
            probs = (weights * (1.0 / total)).astype(BF16)
            probs_ref[a, :, qb : qb + QB] = probs
            parts.append(nn(values_t[a * size : (a + 1) * size], probs))
        heads.append(jnp.concatenate(parts, axis=1))
    mixed_ref[...] = jnp.concatenate(heads, axis=0).T.astype(BF16)


def attend(qkv, lines, fill, head_count):
    length = qkv.shape[0]
    width = qkv.shape[1] // 3
    pairs = head_count // 2
    size = width // pairs

    def column(base):
        return pl.BlockSpec((length, size), lambda p: (0, base + p))

    return call(
        attend_kernel,
        (pairs,),
        [
            column(0),
            column(pairs),
            column(2 * pairs),
            pl.BlockSpec((1, 2, 2 * length), lambda p: (p, 0, 0)),
            whole((length, 1)),
        ],
        [column(0), pl.BlockSpec((2, length, length), lambda p: (p, 0, 0))],
        [shaped((length, width), BF16), shaped((head_count, length, length), BF16)],
        flops=8 * head_count * length * length * size,
    )(qkv, qkv, qkv, lines, fill)


def attend_back_kernel(
    q_ref, k_ref, v_ref, grad_ref, probs_ref, dq_ref, dk_ref, dv_ref, line_ref
):
    length, pair = q_ref.shape
    size = pair // 2
    queries = q_ref[...]
    keys_t = k_ref[...].T
    values = v_ref[...]
    grads = grad_ref[...]
    blocks = length // KB
    dq_heads, dk_heads, dv_heads = [], [], []
    for a in range(2):
        own = jnp.where(head_lanes(grads.shape, a, size), grads, jnp.zeros_like(grads))
        dq_parts = []
        dk = dv = None
        near = {}
        for qb in range(0, length, QB):
            probs = probs_ref[a, :, qb : qb + QB]
            probs_wide = probs.astype(F32)
            pulled = nt(values, own[qb : qb + QB])
            dots = jnp.sum(probs_wide * pulled, axis=0, keepdims=True)
            grad_scores = (probs_wide * (pulled - dots)).astype(BF16)
            dq_parts.append(nn(keys_t[a * size : (a + 1) * size], grad_scores))
            dk_part = nn(grad_scores, queries[qb : qb + QB])
            dv_part = nn(probs, grads[qb : qb + QB])
            dk = dk_part if dk is None else dk + dk_part
            dv = dv_part if dv is None else dv + dv_part
            wide = grad_scores.astype(F32)
            for i in range(blocks):
                for j in range(QB // KB):
                    gap = i - (qb // KB + j)
                    gap = max(-2, min(2, gap))
                    piece = wide[i * KB : (i + 1) * KB, j * KB : (j + 1) * KB]
                    near[gap] = piece if gap not in near else near[gap] + piece
        dq_heads.append(jnp.concatenate(dq_parts, axis=1))
        dk_heads.append(dk)
        dv_heads.append(dv)
        fold = jnp.concatenate([near[1], near[0], near[-1], jnp.zeros_like(near[0])], axis=1)
        rows = KB
        while rows > 8:
            rows //= 2
            fold = fold[:rows] + pltpu.roll(fold[rows : 2 * rows], 4 * KB - rows, 1)
        line_ref[0, a, :, 0 : 4 * KB] = fold
        far = jnp.concatenate([near[2], near[-2]], axis=1)
        line_ref[0, a, :, 4 * KB : 6 * KB] = jnp.sum(far.reshape(KB // 8, 8, 2 * KB), axis=0)
    first = head_lanes(queries.shape, 0, size)
    dq_ref[...] = jnp.concatenate(dq_heads, axis=0).T.astype(BF16)
    dk_ref[...] = jnp.where(first, dk_heads[0], dk_heads[1]).astype(BF16)
    dv_ref[...] = jnp.where(first, dv_heads[0], dv_heads[1]).astype(BF16)


def attend_back(qkv, grad_mixed, probs):
    head_count, length, _ = probs.shape
    width = grad_mixed.shape[1]
    pairs = head_count // 2
    size = width // pairs

    def column(base):
        return pl.BlockSpec((length, size), lambda p: (0, base + p))

    grad_shape = shaped((length, width), BF16)
    return call(
        attend_back_kernel,
        (pairs,),
        [
            column(0),
            column(pairs),
            column(2 * pairs),
            column(0),
            pl.BlockSpec((2, length, length), lambda p: (p, 0, 0)),
        ],
        [
            column(0),
            column(0),
            column(0),
            pl.BlockSpec((1, 2, 8, 6 * KB), lambda p: (p, 0, 0, 0)),
        ],
        [grad_shape, grad_shape, grad_shape, shaped((pairs, 2, 8, 6 * KB), F32)],
        flops=12 * head_count * length * length * size,
    )(qkv, qkv, qkv, grad_mixed, probs)


def line_one_hot(bucket_total):
    column = np.arange(4 * KB)
    rows = []
    for s in range(8):
        place = (column - s) % (4 * KB)
        offset = np.where(place <= 3 * KB, KB - place, 5 * KB - place)
        rows.append(np.concatenate([offset, np.full(KB, 3 * KB), np.full(KB, -3 * KB)]))
    return one_hot_rows(np.concatenate(rows), bucket_total)


def residual_kernel(tokens_ref, mixed_ref, weight_ref, gain_ref, residual_ref, normed_ref):
    residual = tokens_ref[...].astype(F32) + nn(mixed_ref[...], weight_ref[...])
    residual_ref[...] = residual
    normed_ref[...] = (residual * norm_scale(residual) * gain_ref[...]).astype(BF16)


def residual_step(tokens, mixed, weight, gain):
    length, width = tokens.shape
    return call(
        residual_kernel,
        (1,),
        [
            whole((length, width)),
            whole((length, width)),
            whole((width, width)),
            whole((1, width)),
        ],
        [whole((length, width)), whole((length, width))],
        [shaped((length, width), F32), shaped((length, width), BF16)],
        flops=2 * length * width * width,
    )(tokens, mixed, weight, gain)


def feed_kernel(
    normed_ref,
    grad_ref,
    residual_ref,
    gain_ref,
    expand_ref,
    contract_ref,
    out_ref,
    grad_residual_ref,
    grad_low_ref,
    gain_grad_ref,
    expand_grad_ref,
    contract_grad_ref,
    total_ref,
    pulled_ref,
    turned_ref,
):
    step = pl.program_id(0)

    @pl.when(step == 0)
    def _():
        total_ref[...] = residual_ref[...]
        pulled_ref[...] = jnp.zeros_like(pulled_ref)
        turned_ref[...] = normed_ref[...].T

    expand = expand_ref[...]
    contract = contract_ref[...]
    grad_block = grad_ref[...]
    pre = nn(normed_ref[...], expand)
    grad_hidden = nt(grad_block, contract)
    scale = np.float32(np.sqrt(2.0 / np.pi))
    square = pre * pre
    bent = jnp.tanh(pre * (scale + (scale * np.float32(0.044715)) * square))
    half = 0.5 + 0.5 * bent
    hidden = (pre * half).astype(BF16)
    slope = half + (0.5 * pre) * (1.0 - bent * bent) * (
        scale + (scale * np.float32(3 * 0.044715)) * square
    )
    grad_pre = (grad_hidden * slope).astype(BF16)
    total_ref[...] += nn(hidden, contract)
    pulled_ref[...] += nt(grad_pre, expand)
    contract_grad_ref[...] = tn(hidden, grad_block).astype(BF16)
    expand_grad_ref[...] = nn(turned_ref[...], grad_pre).astype(BF16)

    @pl.when(step == pl.num_programs(0) - 1)
    def _():
        out_ref[...] = total_ref[...].astype(BF16)
        grad_values, grad_gain = norm_backward(residual_ref[...], gain_ref[...], pulled_ref[...])
        grad_residual = grad_block.astype(F32) + grad_values
        grad_residual_ref[...] = grad_residual
        grad_low_ref[...] = grad_residual.astype(BF16)
        gain_grad_ref[...] = grad_gain


def feed(normed, grad_block, residual, gain, expand, contract):
    length, width = normed.shape
    hidden = expand.shape[1]
    block = 512
    full = whole((length, width))
    columns = pl.BlockSpec((width, block), lambda j: (0, j))
    rows = pl.BlockSpec((block, width), lambda j: (j, 0))
    return call(
        feed_kernel,
        (hidden // block,),
        [full, full, full, whole((1, width)), columns, rows],
        [full, full, full, whole((1, width)), columns, rows],
        [
            shaped((length, width), BF16),
            shaped((length, width), F32),
            shaped((length, width), BF16),
            shaped((1, width), F32),
            shaped((width, hidden), BF16),
            shaped((hidden, width), BF16),
        ],
        scratch=[
            pltpu.VMEM((length, width), F32),
            pltpu.VMEM((length, width), F32),
            pltpu.VMEM((width, length), BF16),
        ],
        flops=12 * length * width * hidden,
    )(normed, grad_block, residual, gain, expand, contract)


def output_back_kernel(mixed_ref, grad_ref, weight_ref, weight_grad_ref, grad_mixed_ref):
    grad = grad_ref[...]
    grad_mixed_ref[...] = nt(grad, weight_ref[...]).astype(BF16)
    weight_grad_ref[...] = tn(mixed_ref[...], grad).astype(BF16)


def output_back(mixed, grad, weight):
    length, width = mixed.shape
    full = whole((length, width))
    square = whole((width, width))
    return call(
        output_back_kernel,
        (1,),
        [full, full, square],
        [square, full],
        [shaped((width, width), BF16), shaped((length, width), BF16)],
        flops=4 * length * width * width,
    )(mixed, grad, weight)


def project_grad_kernel(normed_ref, dq_ref, dk_ref, dv_ref, out_ref):
    turned = normed_ref[...].T
    width = dq_ref.shape[1]
    for i, ref in enumerate((dq_ref, dk_ref, dv_ref)):
        out_ref[:, i * width : (i + 1) * width] = nn(turned, ref[...]).astype(BF16)


def project_grad(normed, dq, dk, dv):
    length, width = normed.shape
    full = whole((length, width))
    return call(
        project_grad_kernel,
        (1,),
        [full] * 4,
        whole((width, 3 * width)),
        shaped((width, 3 * width), BF16),
        flops=6 * length * width * width,
    )(normed, dq, dk, dv)


def tokens_back_kernel(
    dq_ref, dk_ref, dv_ref, weight_ref, tokens_ref, gain_ref, residual_ref, out_ref, gain_grad_ref
):
    width = dq_ref.shape[1]
    pulled = nt(dq_ref[...], weight_ref[:, 0:width])
    pulled += nt(dk_ref[...], weight_ref[:, width : 2 * width])
    pulled += nt(dv_ref[...], weight_ref[:, 2 * width : 3 * width])
    grad_values, grad_gain = norm_backward(tokens_ref[...].astype(F32), gain_ref[...], pulled)
    out_ref[...] = residual_ref[...] + grad_values
    gain_grad_ref[...] = grad_gain


def tokens_back(dq, dk, dv, weight, tokens, gain, grad_residual):
    length, width = tokens.shape
    full = whole((length, width))
    return call(
        tokens_back_kernel,
        (1,),
        [full, full, full, whole((width, 3 * width)), full, whole((1, width)), full],
        [full, whole((1, width))],
        [shaped((length, width), F32), shaped((1, width), F32)],
        flops=6 * length * width * width,
    )(dq, dk, dv, weight, tokens, gain, grad_residual)


def on_device(
    tokens,
    query_weight,
    key_weight,
    value_weight,
    output_weight,
    expand_weight,
    contract_weight,
    attention_gain,
    feedforward_gain,
    bias_table,
    query_length,
    passage_length,
    pair_order,
    regrouped_grad,
):
    row_count, length, width = tokens.shape
    bucket_count, head_count = bias_table.shape
    narrow_index = lax.axis_index("narrow")
    narrow_count = lax.axis_size("narrow")

    def gathered(weight):
        return lax.all_gather(weight, "wide", axis=0, tiled=True)

    full_qkv = gathered(jnp.concatenate([query_weight, key_weight, value_weight], axis=1))
    full_output = gathered(output_weight)
    full_expand = gathered(expand_weight)
    full_contract = gathered(contract_weight)

    group_rows = regrouped_grad.shape[0]
    chosen = lax.dynamic_slice_in_dim(pair_order, narrow_index * group_rows, group_rows)
    local_rows = chosen // (row_count * narrow_count) * row_count + chosen % row_count
    arranged = jnp.zeros_like(regrouped_grad).at[local_rows].set(regrouped_grad)
    grad_block = lax.all_to_all(arranged, "wide", split_axis=0, concat_axis=1, tiled=True).reshape(
        length, width
    )

    place = np.arange(2 * length)
    offsets = np.where(place <= 2 * length - KB, length - KB - place, 3 * length - KB - place)
    band_hot = jnp.asarray(one_hot_rows(np.clip(offsets, 1 - length, length - 1), bucket_count))
    lines = jnp.dot(bias_table.T, band_hot.T, precision=lax.Precision.HIGHEST)
    lines = lines.reshape(head_count // 2, 2, 2 * length)
    positions = jnp.arange(length, dtype=jnp.int32)
    fill = jnp.where(positions < query_length[0] + passage_length[0], 0.0, negative)
    fill = fill.astype(F32)[:, None]

    inputs = tokens.reshape(length, width)
    gain_one = attention_gain[None]
    gain_two = feedforward_gain[None]
    attention_input, qkv = project(inputs, gain_one, full_qkv)
    mixed, probs = attend(qkv, lines, fill, head_count)
    residual, expand_input = residual_step(inputs, mixed, full_output, gain_two)
    block_output, grad_residual, grad_low, gain_two_grad, expand_grad, contract_grad = feed(
        expand_input, grad_block, residual, gain_two, full_expand, full_contract
    )
    received = lax.all_to_all(
        block_output.reshape(row_count, length, width),
        "wide",
        split_axis=1,
        concat_axis=0,
        tiled=True,
    )
    regrouped = jnp.take(received, local_rows, axis=0)
    output_grad, grad_mixed = output_back(mixed, grad_low, full_output)
    dq, dk, dv, line_grads = attend_back(qkv, grad_mixed, probs)
    qkv_grad = project_grad(attention_input, dq, dk, dv)
    tokens_grad, gain_one_grad = tokens_back(
        dq, dk, dv, full_qkv, inputs, gain_one, grad_residual
    )
    table_grad = jnp.dot(
        jnp.asarray(line_one_hot(bucket_count).T),
        line_grads.reshape(head_count, -1).T,
        precision=lax.Precision.HIGHEST,
    )

    def summed(grad):
        part = lax.psum_scatter(grad, "wide", scatter_dimension=0, tiled=True)
        return lax.psum(part, "narrow").astype(F32)

    final_qkv = summed(qkv_grad)
    final_output = summed(output_grad)
    final_expand = summed(expand_grad)
    final_contract = summed(contract_grad)
    final_attention_gain, final_feedforward_gain, final_table = lax.psum(
        (gain_one_grad[0], gain_two_grad[0], table_grad), ("wide", "narrow")
    )
    return (
        regrouped,
        tokens_grad.reshape(row_count, length, width),
        final_qkv[:, :width],
        final_qkv[:, width : 2 * width],
        final_qkv[:, 2 * width :],
        final_output,
        final_expand,
        final_contract,
        final_attention_gain,
        final_feedforward_gain,
        final_table,
    )


def solution(mesh):
    in_specs = (
        P(("wide", "narrow"), None, None),
        P("wide", None),
        P("wide", None),
        P("wide", None),
        P("wide", None),
        P("wide", None),
        P("wide", None),
        P(),
        P(),
        P(),
        P(("wide", "narrow")),
        P(("wide", "narrow")),
        P(),
        P("narrow", "wide", None),
    )
    out_specs = (
        P("narrow", "wide", None),
        P(("wide", "narrow"), None, None),
        P("wide", None),
        P("wide", None),
        P("wide", None),
        P("wide", None),
        P("wide", None),
        P("wide", None),
        P(),
        P(),
        P(),
    )
    return jax.shard_map(
        on_device, mesh=mesh, in_specs=in_specs, out_specs=out_specs, check_vma=False
    )
```

time: 1350 us -> 734 us (0.54)
  local copies, waits for them, and re-layouts: 307 us -> 11.4 us
  matrix products: 211 us -> 1.29 us
  waiting for transfers between devices: 715 us -> 556 us
  Pallas kernels: 0 us -> 82.3 us
  other arithmetic: 43.1 us -> 14 us
    reduce_scatter x6 -> x4, waiting for transfers between devices: 557 us -> 308 us  [summed(): part = lax.psum_scatter(grad, 'wide', scatter_dimension=0, tiled=True)]
    dot_general x104 -> x2, matrix products: 211 us -> 1.29 us  [the longest x1 0.73 us: on_device(): jnp.dot(jnp.asarray(line_one_hot(bucket_count).T), line_grads.reshape(hea...]
    reshape x36 -> x1, local copies, waits for them, and re-layouts: 102 us -> 0.66 us  [on_device(): lines = lines.reshape(head_count // 2, 2, 2 * length)]
    all_gather x6 -> x4, waiting for transfers between devices: 153 us -> 244 us  [gathered(): return lax.all_gather(weight, 'wide', axis=0, tiled=True)]
    pallas_call x0 -> x8, Pallas kernels: none -> 82.3 us  [the longest x1 22.6 us: feed(): call(feed_kernel, (hidden // block,), [full, full, full, whole((1, width)...]
    slice x72 -> x1, local copies, waits for them, and re-layouts: 82.7 us -> 0.93 us  [on_device(): final_qkv[:, 2 * width:]]
    another operation x48 -> x0, local copies, waits for them, and re-layouts: 45.5 us -> none  [toeplitz_rows(): tiled = jnp.tile(padded, length + 1)]
    while x60 -> x0, local copies, waits for them, and re-layouts: 36.2 us -> none
  transfers between devices with their start and end apart: 15 -> 11, of which waited for: 11 -> 8; matrix products, arithmetic and copies ran while one was open for 17% -> 3% of each run, Pallas kernels for 0% -> 8%
where the time goes in v1:
time: 734 us; the launch traced here: 733 us
  waiting for transfers between devices  556 us (76%)
  Pallas kernels  82.3 us (11%)
  blocking collectives  41.3 us (6%)
  between operations  15.4 us (2%)
  other arithmetic  14 us (2%)
  starting transfers between devices  11.8 us (2%)
  local copies, waits for them, and re-layouts  11.4 us (2%)
    reduce_scatter x4, waiting for transfers between devices, summed(): part = lax.psum_scatter(grad, 'wide', scatter_dimension=0, tiled=True)  308 us
    all_gather x4, waiting for transfers between devices, gathered(): return lax.all_gather(weight, 'wide', axis=0, tiled=True)  244 us
    psum x1, blocking collectives, on_device(): lax.psum((gain_one_grad[0], gain_two_grad[0], table_grad), ('wide', 'narr...  41.3 us
    pallas_call x1, Pallas kernels, feed(): call(feed_kernel, (hidden // block,), [full, full, full, whole((1, width)...  22.6 us
    pallas_call x1, Pallas kernels, attend_back(): call(attend_back_kernel, (pairs,), [column(0), column(pairs), column(2 *...  17.3 us
    pallas_call x1, Pallas kernels, attend(): call(attend_kernel, (pairs,), [column(0), column(pairs), column(2 * pairs...  15.6 us
  transfers between devices with their start and end apart: 11, of which 8 were waited for; matrix products, arithmetic and copies ran while one was open for 3% of the time, Pallas kernels for 8%

profile of v1, /device:TPU:0, one launch (start us, length us, event | category | flops | bytes accessed | tf_op | source)
XLA Modules:
  0.0 733.0 jit_solution(11877802312466193177)
XLA Ops:
  7.3 1.9 pad_maximum_fusion
  9.2 0.7 all-gather.7.cloned.1.call-update
  10.0 0.7 all-gather.11.cloned.1.call-update
  10.7 0.5 all-gather.9.cloned.1.call-update
  11.4 0.9 broadcast_in_dim.36
  12.3 2.7 scatter_fusion
  15.0 7.4 %all-to-all-start = ((bf16[8,64,768]{2,1,0:T(8,128)(2,1)}), bf16[8,64,768]{2,1,0:T(8,128)(2,1)S(1)}, u32[]{:S(2)}, u32[]{:S(2)}) async-start(bf16[8,64,768]{2,1,0:T(8,128)(2,1)} %scatter_fusion), calls=%async_computation | async-start | bytes 1572864 | tf_op jit(solution)/shard_map/all_to_all | solution.py:468
  22.5 0.6 broadcast_in_dim.32.gain_ref
  24.4 0.6 convolution_bitcast_fusion
  24.9 0.7 reshape.64.line_ref
  25.6 0.6 broadcast_in_dim.35.gain_ref
  26.2 0.7 fusion.fill_ref
  26.9 67.2 %all-gather.5.cloned.1.call-done.weight_ref = bf16[768,2304]{1,0:T(8,128)(2,1)} async-done(((bf16[96,2304]{1,0:T(8,128)(2,1)}), bf16[768,2304]{1,0:T(8,128)(2,1)}) %all-gather.5.cloned.1.call-update) | async-done | bytes 3538960 | tf_op jit(solution)/shard_map/all_gather | solution.py:457
  94.1 5.8 shard_map.239
  99.9 15.6 %shard_map.240 = (bf16[512,768]{1,0:T(8,128)(2,1)}, bf16[12,512,512]{2,1,0:T(8,128)(2,1)}) custom-call(bf16[512,2304]{1,0:T(8,128)(2,1)} %get-tuple-element.31.q_ref.k_ref.v_ref, bf16[512,2304]{1,0:T(8,128)(2,1)} %get-tuple-element.31.q_ref.k_ref.v_ref, bf16[512,2304]{1,0:T(8,128)(2,1)} %get-tuple-element.31.q_ref.k_ref.v_ref, ...), custom_call_target="tpu_custom_call" | custom-call | flops 3221225472 | bytes 8388608 | tf_op jit(solution)/shard_map/pallas_call | solution.py:156
  115.5 20.3 %all-gather.7.cloned.1.call-done.weight_ref = bf16[768,768]{1,0:T(8,128)(2,1)} async-done(((bf16[96,768]{1,0:T(8,128)(2,1)}), bf16[768,768]{1,0:T(8,128)(2,1)}) %all-gather.7.cloned.1.call-update) | async-done | bytes 1179664 | tf_op jit(solution)/shard_map/all_gather | solution.py:457
  135.8 4.0 shard_map.241
  139.8 76.9 %all-gather.11.cloned.1.call-done.contract_ref = bf16[3072,768]{1,0:T(8,128)(2,1)} async-done(((bf16[384,768]{1,0:T(8,128)(2,1)}), bf16[3072,768]{1,0:T(8,128)(2,1)}) %all-gather.11.cloned.1.call-update) | async-done | bytes 4718608 | tf_op jit(solution)/shard_map/all_gather | solution.py:457
  216.7 80.1 %all-gather.9.cloned.1.call-done.expand_ref = bf16[768,3072]{1,0:T(8,128)(2,1)} async-done(((bf16[96,3072]{1,0:T(8,128)(2,1)}), bf16[768,3072]{1,0:T(8,128)(2,1)}) %all-gather.9.cloned.1.call-update) | async-done | bytes 4718608 | tf_op jit(solution)/shard_map/all_gather | solution.py:457
  296.8 22.6 %shard_map.242 = (bf16[512,768]{1,0:T(8,128)(2,1)}, f32[512,768]{1,0:T(8,128)}, bf16[512,768]{1,0:T(8,128)(2,1)}, f32[1,768]{1,0:T(1,128)}, bf16[768,3072]{1,0:T(8,128)(2,1)}, /*index=5*/bf16[3072,768]{1,0:T(8,128)(2,1)}) custom-call(bf16[512,768]{1,0:T(8,128)(2,1)} %get-tuple-element.33.normed_ref, bf16[512,768]{1,0:T(8,128)(2,1)} %bitcast.28, ...), custom_call_target="tpu_custom_call" | custom-call | flops 14495514624 | bytes 8388608 | tf_op jit(solution)/shard_map/pallas_call | solution.py:348
  319.4 4.2 shard_map.243
  323.6 0.2 reduce-scatter.5.cloned.1.call-start
  323.9 17.3 %shard_map.244 = (bf16[512,768]{1,0:T(8,128)(2,1)}, bf16[512,768]{1,0:T(8,128)(2,1)}, bf16[512,768]{1,0:T(8,128)(2,1)}, f32[6,2,8,768]{3,2,1,0:T(8,128)}) custom-call(bf16[512,2304]{1,0:T(8,128)(2,1)} %get-tuple-element.31.q_ref.k_ref.v_ref, bf16[512,2304]{1,0:T(8,128)(2,1)} %get-tuple-element.31.q_ref.k_ref.v_ref, ...), custom_call_target="tpu_custom_call" | custom-call | flops 4831838208 | bytes 8388608 | tf_op jit(solution)/shard_map/pallas_call | solution.py:233
  341.1 5.7 shard_map.246
  346.9 0.7 reduce-scatter.11.cloned.1.call-update
  347.7 0.7 reduce-scatter.9.cloned.1.call-update
  348.4 0.4 copy-done.6
  348.8 1.2 copy.32
  350.0 0.5 broadcast.62
  350.5 5.4 reduce.2
  356.0 1.1 reshape.89
  357.0 3.7 all-to-all-start.1
  360.7 0.3 all-reduce.4.cloned.1.call-start
  361.0 28.8 %reduce-scatter.7.cloned.1.call-done = bf16[96,768]{1,0:T(8,128)(2,1)} async-done(((bf16[768,768]{1,0:T(8,128)(2,1)}), bf16[96,768]{1,0:T(8,128)(2,1)}) %reduce-scatter.7.cloned.1.call-update) | async-done | bytes 147472 | tf_op jit(solution)/shard_map/reduce_scatter | solution.py:511
  389.8 81.8 %reduce-scatter.5.cloned.1.call-done = bf16[96,2304]{1,0:T(8,128)(2,1)} async-done(((bf16[768,2304]{1,0:T(8,128)(2,1)}), bf16[96,2304]{1,0:T(8,128)(2,1)}) %reduce-scatter.5.cloned.1.call-update) | async-done | bytes 442384 | tf_op jit(solution)/shard_map/reduce_scatter | solution.py:511
  471.6 98.5 %reduce-scatter.11.cloned.1.call-done = bf16[384,768]{1,0:T(8,128)(2,1)} async-done(((bf16[3072,768]{1,0:T(8,128)(2,1)}), bf16[384,768]{1,0:T(8,128)(2,1)}) %reduce-scatter.11.cloned.1.call-update) | async-done | bytes 589840 | tf_op jit(solution)/shard_map/reduce_scatter | solution.py:511
  570.1 98.7 %reduce-scatter.9.cloned.1.call-done = bf16[96,3072]{1,0:T(8,128)(2,1)} async-done(((bf16[768,3072]{1,0:T(8,128)(2,1)}), bf16[96,3072]{1,0:T(8,128)(2,1)}) %reduce-scatter.9.cloned.1.call-update) | async-done | bytes 589840 | tf_op jit(solution)/shard_map/reduce_scatter | solution.py:511
  669.0 7.1 shard_map.245
  676.1 0.7 reduce
  676.9 0.7 fusion.2
  677.6 41.3 %all-reduce = (f32[768]{0:T(1024)}, f32[768]{0:T(1024)}, f32[32,12]{0,1:T(8,128)}) all-reduce(f32[768]{0:T(1024)S(1)} %reduce, f32[768]{0:T(1024)S(1)} %reduce.1, f32[32,12]{0,1:T(8,128)S(1)} %fusion.2), channel_id=1, replica_groups=mesh['wide'=8,'narrow'=4] {'wide','narrow'}, use_global_device_ids=true, to_apply=%region_9.10 | all-reduce | flops 1920 | bytes 15360 | tf_op jit(solution)/shard_map/psum | solution.py:518
  718.9 0.8 reshape.90
  719.8 0.6 gather_fusion
  720.4 1.0 broadcast_select_fusion
  721.5 2.3 convert_element_type.14
  723.7 1.1 convert_element_type.15
  724.8 0.9 fusion.1
  725.7 0.7 convert_element_type.13
  (49 shorter events, 0.8 us)
Async XLA Ops:
  7.2 17.2 %copy-start = (f32[32,12]{0,1:T(8,128)S(1)}, f32[32,12]{0,1:T(8,128)}, u32[]{:S(2)}) copy-start(f32[32,12]{0,1:T(8,128)} %param.25) | copy-start | bytes 4612
  7.2 4.1 copy-start.14
  7.2 5.1 copy-start.3
  7.2 86.9 %all-gather.5.cloned.1.call-start = ((), (), s32[]{:S(2)}) async-start(), calls=%async_computation.6 | async-start | bytes 3981312 | tf_op jit(solution)/shard_map/all_gather | solution.py:457
  9.2 126.6 %all-gather.7.cloned.1.call-start = ((), (), s32[]{:S(2)}) async-start(), calls=%async_computation.7 | async-start | bytes 1327104 | tf_op jit(solution)/shard_map/all_gather | solution.py:457
  9.9 206.7 %all-gather.11.cloned.1.call-start = ((), (), s32[]{:S(2)}) async-start(), calls=%async_computation.9 | async-start | bytes 5308416 | tf_op jit(solution)/shard_map/all_gather | solution.py:457
  10.7 286.1 %all-gather.9.cloned.1.call-start = ((), (), s32[]{:S(2)}) async-start(), calls=%async_computation.8 | async-start | bytes 5308416 | tf_op jit(solution)/shard_map/all_gather | solution.py:457
  12.3 10.1 %copy-start.11 = (f32[768]{0:T(1024)S(1)}, f32[768]{0:T(1024)}, u32[]{:S(2)}) copy-start(f32[768]{0:T(1024)} %param.23) | copy-start | bytes 9220
  12.3 12.0 %copy-start.8 = (f32[1024,32]{1,0:T(8,128)S(1)}, f32[1024,32]{1,0:T(8,128)}, u32[]{:S(2)}) copy-start(f32[1024,32]{1,0:T(8,128)} %constant.64.clone) | copy-start | bytes 393220
  15.0 10.6 %copy-start.12 = (f32[768]{0:T(1024)S(1)}, f32[768]{0:T(1024)}, u32[]{:S(2)}) copy-start(f32[768]{0:T(1024)} %param.24) | copy-start | bytes 9220
  15.0 124.8 %all-to-all-start = ((bf16[8,64,768]{2,1,0:T(8,128)(2,1)}), bf16[8,64,768]{2,1,0:T(8,128)(2,1)S(1)}, u32[]{:S(2)}, u32[]{:S(2)}) async-start(bf16[8,64,768]{2,1,0:T(8,128)(2,1)} %scatter_fusion), calls=%async_computation | async-start | bytes 1572864 | tf_op jit(solution)/shard_map/all_to_all | solution.py:468
  22.4 367.4 %reduce-scatter.7.cloned.1.call-start = ((), (), s32[]{:S(2)}) async-start(), calls=%async_computation.11 | async-start | bytes 1327104 | tf_op jit(solution)/shard_map/reduce_scatter | solution.py:511
  139.8 157.0 %copy-start.5 = (bf16[8,64,768]{2,1,0:T(8,128)(2,1)}, bf16[8,64,768]{2,1,0:T(8,128)(2,1)S(1)}, u32[]{:S(2)}) copy-start(bf16[8,64,768]{2,1,0:T(8,128)(2,1)S(1)} %all-to-all-done) | copy-start | bytes 2359300
  323.6 148.0 %reduce-scatter.5.cloned.1.call-start = ((), (), s32[]{:S(2)}) async-start(), calls=%async_computation.10 | async-start | bytes 3981312 | tf_op jit(solution)/shard_map/reduce_scatter | solution.py:511
  346.9 223.2 %reduce-scatter.11.cloned.1.call-start = ((), (), s32[]{:S(2)}) async-start(), calls=%async_computation.13 | async-start | bytes 5308416 | tf_op jit(solution)/shard_map/reduce_scatter | solution.py:511
  347.6 321.2 %reduce-scatter.9.cloned.1.call-start = ((), (), s32[]{:S(2)}) async-start(), calls=%async_computation.12 | async-start | bytes 5308416 | tf_op jit(solution)/shard_map/reduce_scatter | solution.py:511
  347.7 1.1 copy-start.6
  357.0 311.8 %copy-start.9 = (f32[6,2,8,768]{3,2,1,0:T(8,128)S(1)}, f32[6,2,8,768]{3,2,1,0:T(8,128)}, u32[]{:S(2)}) copy-start(f32[6,2,8,768]{3,2,1,0:T(8,128)} %get-tuple-element.50) | copy-start | bytes 884740
  357.0 361.9 %all-to-all-start.1 = ((bf16[8,2,24576]{2,1,0:T(2,128)(2,1)}), bf16[8,2,24576]{2,1,0:T(2,128)(2,1)S(1)}, u32[]{:S(2)}, u32[]{:S(2)}) async-start(bf16[8,2,24576]{2,1,0:T(2,128)(2,1)} %reshape.89), calls=%async_computation.1 | async-start | bytes 1572864 | tf_op jit(solution)/shard_map/all_to_all | solution.py:490
  360.7 360.7 %all-reduce.4.cloned.1.call-start = ((), (), s32[]{:S(2)}) async-start(), calls=%async_computation.14 | async-start | bytes 3538944 | tf_op jit(solution)/shard_map/psum | solution.py:512
  669.0 7.8 %copy-start.13 = (f32[1,768]{1,0:T(1,128)S(1)}, f32[1,768]{1,0:T(1,128)}, u32[]{:S(2)}) copy-start(f32[1,768]{1,0:T(1,128)} %get-tuple-element.49) | copy-start | bytes 9220
  669.0 7.8 %copy-start.4 = (f32[32,6144]{1,0:T(8,128)S(1)}, f32[32,6144]{1,0:T(8,128)}, u32[]{:S(2)}) copy-start(f32[32,6144]{1,0:T(8,128)} %constant.65.clone) | copy-start | bytes 2359300
  721.4 2.3 copy-start.7
  721.5 3.4 copy-start.2
  723.7 2.8 copy-start.1
  723.7 2.0 copy-start.10
Sparse Core Ops, SparseCore 0:
  10.8 83.2 all-gather.4
  96.3 39.5 all-gather.6
  138.0 78.6 all-gather.10
  218.7 78.0 all-gather.8
  323.8 65.9 reduce-scatter.6
  393.3 78.3 reduce-scatter.4
  475.2 94.8 reduce-scatter.10
  573.7 95.0 reduce-scatter.8
  671.4 47.7 all-reduce.3
